TPU v7x, 256 devices: a whole 4x4x8 slice. The times are simulated.
256 devices in a mesh: child: 2 (over core), row: 8 (over z), col: 16 (over x, y).
Axes of the slice: x: 4, y: 4, z: 8, core: 2. Of those that a mesh axis runs over, the one named last changes fastest.
Arguments:
- parent_slab: float32 [3072, 61440], P('col', ('child', 'row')), may hold values from -6 to 6
- panel: float32 [2, 16384, 1024], P('child', 'row'), may hold values from -0.0625 to 0.0625
- slab_panel: float32 [2, 3072, 1024], P('child', 'col'), may hold values from -0.15625 to 0.15625
- diag_inverse: float32 [2, 1024, 1024], P('child', 'col', 'row'), may hold values from -6 to 6
- tile_rows: int32 [2, 128, 128], replicated, may hold values from -1 to 3839, as said below
- tile_owner: int32 [2, 128, 1], replicated, may hold values from 0 to 15; in each aligned block of 16 rows (0 to 15, 16 to 31, ..., all dimensions but the last counted through in order) at most 2 rows name the same one
Outputs:
- slab_inverse: float32 [2, 3072, 1024], P('child', 'col', 'row')
- diag_block: float32 [2, 1024, 1024], P('child', 'col', 'row')
Inputs may be any that keep to these rules, and one draw needn't show every extreme that they name: `tile_rows`: A tile's offsets lie in the column block of its owner; -1 marks padding and fills only the end of a tile. `tile_owner`: among the 16 tiles of one device (aligned blocks of one child), no owner holds more than 2.
All inputs are finite; a program needn't handle non-finite values.
Results may differ from a plain program's by a relative error of at most 0.0001.
Values sent between devices are 32-bit elements; how exact they have to be, the bound alone decides.
No kernel may reach another device: no remote copies, remote signals or barrier semaphores. Data moves between devices by JAX's collectives and lax.ppermute only.
A program may use at most 128 MiB of HBM per device.

v0:
```python
import jax
import jax.numpy as jnp
from jax import lax
from jax.sharding import PartitionSpec as P

CAP = 2


def rank_tiles(blocks):
    tile_count = blocks.shape[1]
    same_owner = blocks[:, :, None] == blocks[:, None, :]
    earlier = lax.broadcasted_iota(jnp.int32, (tile_count, tile_count), 1) < lax.broadcasted_iota(
        jnp.int32, (tile_count, tile_count), 0
    )
    return jnp.sum((same_owner & earlier[None]).astype(jnp.int32), axis=2)


def choose(matches):
    positions = jnp.arange(matches.shape[-1], dtype=jnp.int32)
    chosen = jnp.sum(jnp.where(matches, positions, 0), axis=-1)
    return (chosen, jnp.any(matches, axis=-1))


def owned_columns(parent_slab, blocks, ranks, offsets, my_block, slots):
    slot_ids = jnp.arange(slots, dtype=jnp.int32)
    matches = (blocks[:, None, :] == my_block) & (ranks[:, None, :] == slot_ids[None, :, None])
    chosen, present = choose(matches)
    spread = jnp.broadcast_to(chosen[:, :, None], chosen.shape + (offsets.shape[2],))
    picked = jnp.take_along_axis(offsets, spread, axis=1)
    usable = present[:, :, None] & (picked >= 0)
    flat_cols = jnp.where(usable, picked, 0).reshape(-1)
    columns = jnp.take(parent_slab, flat_cols, axis=1)
    return columns * usable.reshape(-1).astype(jnp.float32)[None, :]


def local(parent_slab, panel, slab_panel, diag_inverse, tile_rows, tile_owner):
    group_size = lax.axis_size("child") * lax.axis_size("row")
    my_block = lax.axis_index("child") * lax.axis_size("row") + lax.axis_index("row")
    tile_len = tile_rows.shape[2]
    blocks = tile_owner.reshape(group_size, -1)
    tile_count = blocks.shape[1]
    offsets = tile_rows.reshape(group_size, tile_count, tile_len)
    ranks = rank_tiles(blocks)
    own_blocks = lax.dynamic_index_in_dim(blocks, my_block, 0, keepdims=False)
    own_ranks = lax.dynamic_index_in_dim(ranks, my_block, 0, keepdims=False)
    tiles_here = panel[0]
    slab_rows = parent_slab.shape[0]
    panel_width = panel.shape[2]
    slot_ids = jnp.arange(CAP, dtype=jnp.int32)
    owners = jnp.arange(group_size, dtype=jnp.int32)
    matches = (own_blocks[None, None, :] == owners[:, None, None]) & (
        own_ranks[None, None, :] == slot_ids[None, :, None]
    )
    chosen, present = choose(matches)
    outgoing = jnp.take(
        tiles_here.reshape(tile_count, tile_len, panel_width), chosen.reshape(-1), axis=0
    )
    outgoing = outgoing * present.reshape(-1, 1, 1).astype(jnp.float32)
    outgoing = outgoing.reshape(group_size * CAP * tile_len, panel_width)
    arrived = lax.all_to_all(outgoing, ("child", "row"), split_axis=0, concat_axis=0, tiled=True)
    columns = owned_columns(parent_slab, blocks, ranks, offsets, my_block, CAP)
    child_count = lax.axis_size("child")
    partial_value = -jnp.einsum(
        "rcm,cmb->rcb",
        columns.reshape(slab_rows, child_count, -1),
        arrived.reshape(child_count, -1, panel_width),
        precision=lax.Precision.HIGHEST,
    )
    slab_inverse = lax.psum_scatter(
        partial_value.reshape(slab_rows, child_count * panel_width),
        ("child", "row"),
        scatter_dimension=1,
        tiled=True,
    )
    diag_terms = lax.dot_general(
        slab_panel[0],
        slab_inverse,
        (((0,), (0,)), ((), ())),
        precision=lax.Precision.HIGHEST,
        preferred_element_type=jnp.float32,
    )
    reduced = lax.psum_scatter(diag_terms, "col", scatter_dimension=0, tiled=True)
    diag_block = diag_inverse[0] - reduced
    return (slab_inverse[None], diag_block[None])


def solution(mesh):
    in_specs = (
        P("col", ("child", "row")),
        P("child", "row", None),
        P("child", "col", None),
        P("child", "col", "row"),
        P(),
        P(),
    )
    out_specs = (P("child", "col", "row"), P("child", "col", "row"))
    return jax.shard_map(local, mesh=mesh, in_specs=in_specs, out_specs=out_specs, check_vma=False)
```

profile of v0, /device:TPU:8, one launch (start us, length us, event | category | flops | bytes accessed | tf_op | source)
XLA Modules:
  0.0 576.9 jit_solution(4964308816868313071)
XLA Ops:
  7.2 0.5 broadcast.278
  7.7 1.3 reduce.3
  9.1 0.4 convert_reduce_fusion
  9.6 0.1 fusion.11
  9.8 0.1 and_reduce_fusion
  10.5 11.5 %gather_fusion = f32[32,128,1024]{2,1,0:T(8,128)} fusion(f32[16,128,1024]{2,1,0:T(8,128)} %bitcast.52, s32[1024]{0:T(1024)S(1)} %pad_clamp_fusion), kind=kCustom, calls=%fused_computation | custom fusion | bytes 33554560 | tf_op jit(solution)/shard_map/jit(_take)/gather | solution.py:55
  21.9 11.6 %fusion = f32[16,256,1024]{2,1,0:T(8,128)} fusion(f32[16,256]{1,0:T(8,128)S(1)} %bitcast.57, pred[16,256]{1,0:T(8,128)(4,1)S(1)} %bitcast.62, f32[16,256,1024]{2,1,0:T(8,128)} %bitcast.51), kind=kLoop, calls=%fused_computation.4 | loop fusion | flops 8388608 | bytes 33574912 | tf_op jit(solution)/shard_map/mul | solution.py:58
  33.5 8.6 %all-to-all-start = ((f32[16,256,1024]{2,1,0:T(8,128)}), f32[16,256,1024]{2,1,0:T(8,128)}, u32[]{:S(2)}, u32[]{:S(2)}) async-start(f32[16,256,1024]{2,1,0:T(8,128)} %fusion), calls=%async_computation | async-start | bytes 33554432 | tf_op jit(solution)/shard_map/all_to_all | solution.py:60
  42.2 0.1 fusion.13
  43.0 5.0 copy.32
  48.0 0.1 shift-left_or_fusion
  48.1 33.2 %gather_fusion.2 = s32[4096]{0:T(1024)S(1)} fusion(s32[16,16,128]{2,1,0:T(8,128)S(1)} %bitcast.49, s32[4096]{0:T(1024)S(1)} %bitcast.50), kind=kCustom, calls=%fused_computation.2 | custom fusion | bytes 81920 | tf_op jit(solution)/shard_map/jit(take_along_axis)/gather | solution.py:29
  81.3 0.1 and_select_fusion.1
  81.5 18.2 %gather_fusion.1 = f32[4096,192]{1,0:T(8,128)} fusion(f32[192,3840]{0,1:T(8,128)} %copy.32, s32[4096]{0:T(1024)S(1)} %broadcast_clamp_fusion), kind=kCustom, calls=%fused_computation.1 | custom fusion | bytes 6307840 | tf_op jit(solution)/shard_map/jit(_take)/gather | solution.py:32
  99.7 5.2 copy.33
  105.0 301.7 %all-to-all-done = f32[16,256,1024]{2,1,0:T(8,128)} async-done(((f32[16,256,1024]{2,1,0:T(8,128)}), f32[16,256,1024]{2,1,0:T(8,128)}, u32[]{:S(2)}, u32[]{:S(2)}) %all-to-all-start) | async-done | bytes 16777248 | tf_op jit(solution)/shard_map/all_to_all | solution.py:60
  406.7 16.2 %negate_bitcast_fusion = f32[2,24,8,1024]{3,2,1,0:T(8,128)S(1)} fusion(f32[2,2048,1024]{2,1,0:T(8,128)} %bitcast.5, f32[192,2,2048]{2,0,1:T(8,128)} %copy.33, f32[2,2048]{1,0:T(2,128)S(1)} %get-tuple-element.11, pred[2,2048]{1,0:T(4,128)(4,1)S(1)} %get-tuple-element.10), kind=kOutput, calls=%fused_computation.8 | convolution fusion | flops 9665642496 | bytes 21516288 | tf_op jit(solution)/shard_map/rcm,cmb->rcb/dot_general | solution.py:63
  422.9 1.3 copy.39
  424.3 62.9 %reduce-scatter.5.cloned.1.call-done = f32[192,128]{1,0:T(8,128)} async-done(((f32[192,2048]{1,0:T(8,128)}), f32[192,128]{1,0:T(8,128)}) %reduce-scatter.5.cloned.1.call-update) | async-done | bytes 98320 | tf_op jit(solution)/shard_map/reduce_scatter | solution.py:69
  487.2 1.5 convolution_bitcast_fusion
  488.7 1.0 copy.37
  489.9 78.6 %reduce-scatter.7.cloned.1.call-done = f32[64,128]{1,0:T(8,128)} async-done(((f32[1024,128]{1,0:T(8,128)}), f32[64,128]{1,0:T(8,128)}) %reduce-scatter.7.cloned.1.call-update) | async-done | bytes 32784
  568.5 0.8 copy.38
  569.4 0.7 copy.36
  (44 shorter events, 1.7 us)
Async XLA Ops:
  7.2 480.0 %copy-start = (f32[1,192,1024]{2,1,0:T(8,128)S(1)}, f32[1,192,1024]{2,1,0:T(8,128)}, u32[]{:S(2)}) copy-start(f32[1,192,1024]{2,1,0:T(8,128)} %param.8) | copy-start | bytes 2359300
  33.5 373.2 %all-to-all-start = ((f32[16,256,1024]{2,1,0:T(8,128)}), f32[16,256,1024]{2,1,0:T(8,128)}, u32[]{:S(2)}, u32[]{:S(2)}) async-start(f32[16,256,1024]{2,1,0:T(8,128)} %fusion), calls=%async_computation | async-start | bytes 33554432 | tf_op jit(solution)/shard_map/all_to_all | solution.py:60
  42.1 445.1 %reduce-scatter.5.cloned.1.call-start = ((), (), s32[]{:S(2)}) async-start(), calls=%async_computation.3 | async-start | bytes 1671168 | tf_op jit(solution)/shard_map/reduce_scatter | solution.py:69
  43.0 5.1 copy-start.1
  422.9 66.9 %copy-start.2 = (f32[1,64,128]{2,1,0:T(8,128)S(1)}, f32[1,64,128]{2,1,0:T(8,128)}, u32[]{:S(2)}) copy-start(f32[1,64,128]{2,1,0:T(8,128)} %param.9) | copy-start | bytes 98308
  424.2 144.3 %reduce-scatter.7.cloned.1.call-start = ((), (), s32[]{:S(2)}) async-start(), calls=%async_computation.4 | async-start | bytes 557056
Sparse Core Ops, SparseCore 0:
  424.3 62.8 reduce-scatter.4
  491.1 77.3 reduce-scatter.6
where the time goes:
time: 577 us
  waiting for transfers between devices  443 us (77%)
  local copies, waits for them, and re-layouts  78.7 us (14%)
  matrix products  17.7 us (3%)
  between operations  14.3 us (2%)
  other arithmetic  14.2 us (2%)
  starting transfers between devices  8.7 us (2%)
    all_to_all x1, waiting for transfers between devices, local(): lax.all_to_all(outgoing, ('child', 'row'), split_axis=0, concat_axis=0, t...  302 us
    unnamed x3, waiting for transfers between devices  78.7 us
    reduce_scatter x1, waiting for transfers between devices, local(): lax.psum_scatter(partial_value.reshape(slab_rows, child_count * panel_wid...  62.9 us
    gather x1, local copies, waits for them, and re-layouts, owned_columns(): picked = jnp.take_along_axis(offsets, spread, axis=1)  33.2 us
    gather x2, local copies, waits for them, and re-layouts, owned_columns(): columns = jnp.take(parent_slab, flat_cols, axis=1)  23.4 us
    dot_general x1, matrix products, local(): jnp.einsum('rcm,cmb->rcb', columns.reshape(slab_rows, child_count, -1), a...  16.2 us
    mul x1, other arithmetic, local(): outgoing = outgoing * present.reshape(-1, 1, 1).astype(jnp.float32)  11.6 us
  transfers between devices with their start and end apart: 3, of which 3 were waited for; matrix products, arithmetic and copies ran while one was open for 11% of the time, Pallas kernels for 0%

commit v1 on v0

v1 whole, which is shorter than its diff:
```python
import jax
import jax.numpy as jnp
from jax import lax
from jax.experimental import pallas as pl
from jax.experimental.pallas import tpu as pltpu
from jax.sharding import PartitionSpec as P

CAP = 2
VMEM_LIMIT = 48 << 20


def split(value):
    high = value.astype(jnp.bfloat16)
    low = (value - high.astype(jnp.float32)).astype(jnp.bfloat16)
    return high, low


def dot(left, right, contract=((1,), (0,))):
    return lax.dot_general(left, right, (contract, ((), ())), preferred_element_type=jnp.float32)


def gather_kernel(owner, me, rows, slab, out, parts, tiles, slots):
    slab_rows, width = slab.shape
    blocks, count = owner.shape
    high, low = split(slab[...])
    parts[0:slab_rows, :] = high
    parts[slab_rows:, :] = low
    mine = me[0]

    def block_scan(block, found):
        def tile_scan(tile, carry):
            found, rank = carry
            hit = (owner[block, tile] == mine).astype(jnp.int32)
            tiles[found] = block * count + tile
            slots[found] = block * CAP + rank
            return found + hit, rank + hit

        return lax.fori_loop(0, count, tile_scan, (found, 0))[0]

    found = lax.fori_loop(0, blocks, block_scan, 0)
    tiles[found] = 0
    chunk = width // 5

    def pair(step, carry):
        first = 2 * step
        second = first + 1
        columns = jnp.concatenate([rows[pl.ds(tiles[first], 1), :], rows[pl.ds(tiles[second], 1), :]], axis=1)
        total = jnp.zeros((2 * slab_rows, columns.shape[1]), jnp.float32)
        for begin in range(0, width, chunk):
            places = lax.broadcasted_iota(jnp.int32, (chunk, columns.shape[1]), 0) + begin
            picks = jnp.where(places == columns, 1.0, 0.0).astype(jnp.bfloat16)
            total += dot(parts[:, begin : begin + chunk], picks)
        total = total[:slab_rows] + total[slab_rows:]
        half = columns.shape[1] // 2
        out[slots[first]] = total[:, :half]

        @pl.when(second < found)
        def _():
            out[slots[second]] = total[:, half:]

        return carry

    lax.fori_loop(0, (found + 1) // 2, pair, 0)


def gather(parent_slab, rows, owner, me):
    slab_rows, width = parent_slab.shape
    blocks, count = owner.shape
    tile_len = rows.shape[1]
    smem = pl.BlockSpec(memory_space=pltpu.SMEM)
    vmem = pl.BlockSpec(memory_space=pltpu.VMEM)
    return pl.pallas_call(
        gather_kernel,
        out_shape=jax.ShapeDtypeStruct((blocks * CAP, slab_rows, tile_len), jnp.float32),
        in_specs=[smem, smem, vmem, vmem],
        out_specs=vmem,
        scratch_shapes=[
            pltpu.VMEM((2 * slab_rows, width), jnp.bfloat16),
            pltpu.SMEM((blocks * CAP + 8,), jnp.int32),
            pltpu.SMEM((blocks * CAP + 8,), jnp.int32),
        ],
        compiler_params=pltpu.CompilerParams(vmem_limit_bytes=VMEM_LIMIT),
    )(owner, me, rows, parent_slab)


def product_kernel(owner, me, arrived, panel, out, total):
    step = pl.program_id(0)
    count = owner.shape[1]
    mine = me[0]

    def slot_of(tile):
        own = owner[mine, tile]

        def earlier(other, rank):
            return rank + jnp.where((owner[mine, other] == own) & (other < tile), 1, 0)

        return own * CAP + lax.fori_loop(0, count, earlier, 0)

    left = jnp.concatenate([arrived[slot_of(2 * step)], arrived[slot_of(2 * step + 1)]], axis=1)
    left_high, left_low = split(left)
    right_high, right_low = split(panel[...])
    term = dot(left_high, right_high) + dot(left_high, right_low) + dot(left_low, right_high)

    @pl.when(step == 0)
    def _():
        total[...] = -term

    @pl.when(step > 0)
    def _():
        total[...] -= term

    @pl.when(step == pl.num_programs(0) - 1)
    def _():
        width = out.shape[2]
        for block in range(out.shape[0]):
            out[block] = total[:, block * width : (block + 1) * width]


def product(arrived, panel, owner, me, blocks):
    slots, slab_rows, tile_len = arrived.shape
    panel_rows, width = panel.shape
    smem = pl.BlockSpec(memory_space=pltpu.SMEM)
    out_shape = (blocks, slab_rows, width // blocks)
    return pl.pallas_call(
        product_kernel,
        grid=(panel_rows // (2 * tile_len),),
        out_shape=jax.ShapeDtypeStruct(out_shape, jnp.float32),
        in_specs=[
            smem,
            smem,
            pl.BlockSpec(arrived.shape, lambda i: (0, 0, 0)),
            pl.BlockSpec((2 * tile_len, width), lambda i: (i, 0)),
        ],
        out_specs=pl.BlockSpec(out_shape, lambda i: (0, 0, 0)),
        scratch_shapes=[pltpu.VMEM((slab_rows, width), jnp.float32)],
        compiler_params=pltpu.CompilerParams(vmem_limit_bytes=VMEM_LIMIT),
    )(owner, me, arrived, panel)


def diag_kernel(terms, slab_panel, inverse, out):
    total = jnp.sum(terms[...], axis=0)
    inverse[...] = total
    right_high, right_low = split(total)
    left_high, left_low = split(slab_panel[...])
    both = ((0,), (0,))
    result = dot(left_high, right_high, both) + dot(left_high, right_low, both) + dot(left_low, right_high, both)
    out[...] = result.reshape(out.shape)


def diag_terms(terms, slab_panel, blocks):
    _, slab_rows, width = terms.shape
    rows = slab_panel.shape[1]
    vmem = pl.BlockSpec(memory_space=pltpu.VMEM)
    return pl.pallas_call(
        diag_kernel,
        out_shape=(
            jax.ShapeDtypeStruct((slab_rows, width), jnp.float32),
            jax.ShapeDtypeStruct((blocks, rows // blocks, width), jnp.float32),
        ),
        in_specs=[vmem, vmem],
        out_specs=(vmem, vmem),
        compiler_params=pltpu.CompilerParams(vmem_limit_bytes=VMEM_LIMIT),
    )(terms, slab_panel)


def local(parent_slab, panel, slab_panel, diag_inverse, tile_rows, tile_owner):
    row_count, col_count = lax.axis_size("row"), lax.axis_size("col")
    group_size = lax.axis_size("child") * row_count
    me = (lax.axis_index("child") * row_count + lax.axis_index("row")).astype(jnp.int32).reshape(1)
    owner = tile_owner.reshape(group_size, -1)
    rows = tile_rows.reshape(-1, tile_rows.shape[2])
    columns = gather(parent_slab, rows, owner, me)
    arrived = lax.all_to_all(columns, ("child", "row"), split_axis=0, concat_axis=0, tiled=True)
    partial = product(arrived, panel[0], owner, me, row_count)
    terms = lax.all_to_all(partial, "row", split_axis=0, concat_axis=0, tiled=True)
    slab_inverse, parts = diag_terms(terms, slab_panel[0], col_count)
    reduced = lax.all_to_all(parts, "col", split_axis=0, concat_axis=0, tiled=True)
    diag_block = diag_inverse[0] - jnp.sum(reduced, axis=0)
    return slab_inverse[None], diag_block[None]


def solution(mesh):
    in_specs = (
        P("col", ("child", "row")),
        P("child", "row", None),
        P("child", "col", None),
        P("child", "col", "row"),
        P(),
        P(),
    )
    out_specs = (P("child", "col", "row"), P("child", "col", "row"))
    return jax.shard_map(local, mesh=mesh, in_specs=in_specs, out_specs=out_specs, check_vma=False)
```

time: 577 us -> 161 us (0.28)
  waiting for transfers between devices: 443 us -> 0 us
  blocking collectives: 0 us -> 131 us
  local copies, waits for them, and re-layouts: 78.7 us -> 3.34 us
  Pallas kernels: 0 us -> 23.5 us
  matrix products: 17.7 us -> 0 us
  between operations: 14.3 us -> 0.67 us
  other arithmetic: 14.2 us -> 2 us
  starting transfers between devices: 8.7 us -> 0 us
    all_to_all x1 -> x0, waiting for transfers between devices: 302 us -> none  [local(): lax.all_to_all(outgoing, ('child', 'row'), split_axis=0, concat_axis=0, t...]
    all_to_all x0 -> x3, blocking collectives: none -> 131 us  [the longest x1 87.7 us: local(): lax.all_to_all(columns, ('child', 'row'), split_axis=0, concat_axis=0, ti...]
    unnamed x3 -> x0, waiting for transfers between devices: 78.7 us -> none
    gather x4 -> x0, local copies, waits for them, and re-layouts: 68.1 us -> none  [the longest x1 33.2 us: owned_columns(): picked = jnp.take_along_axis(offsets, spread, axis=1)]
    reduce_scatter x1 -> x0, waiting for transfers between devices: 62.9 us -> none  [local(): lax.psum_scatter(partial_value.reshape(slab_rows, child_count * panel_wid...]
    pallas_call x0 -> x3, Pallas kernels: none -> 23.5 us  [the longest x1 13 us: gather(): pl.pallas_call(gather_kernel, out_shape=jax.ShapeDtypeStruct((blocks * CA...]
    dot_general x2 -> x0, matrix products: 17.7 us -> none  [the longest x1 16.2 us: local(): jnp.einsum('rcm,cmb->rcb', columns.reshape(slab_rows, child_count, -1), a...]
    mul x1 -> x0, other arithmetic: 11.6 us -> none  [local(): outgoing = outgoing * present.reshape(-1, 1, 1).astype(jnp.float32)]
  transfers between devices with their start and end apart: 3 -> 0, of which waited for: 3 -> 0; matrix products, arithmetic and copies ran while one was open for 11% -> 0% of each run, Pallas kernels for 0% -> 0%
where the time goes in v1:
time: 161 us
  blocking collectives  131 us (81%)
  Pallas kernels  23.5 us (15%)
  local copies, waits for them, and re-layouts  3.34 us (2%)
  other arithmetic  2 us (1%)
    all_to_all x1, blocking collectives, local(): lax.all_to_all(columns, ('child', 'row'), split_axis=0, concat_axis=0, ti...  87.7 us
    all_to_all x1, blocking collectives, local(): lax.all_to_all(partial, 'row', split_axis=0, concat_axis=0, tiled=True)  27.5 us
    all_to_all x1, blocking collectives, local(): lax.all_to_all(parts, 'col', split_axis=0, concat_axis=0, tiled=True)  16 us
    pallas_call x1, Pallas kernels, gather(): pl.pallas_call(gather_kernel, out_shape=jax.ShapeDtypeStruct((blocks * CA...  13 us
    pallas_call x1, Pallas kernels, product(): pl.pallas_call(product_kernel, grid=(panel_rows // (2 * tile_len),), out_...  9.8 us
    unnamed x9, local copies, waits for them, and re-layouts  3.26 us

profile of v1, /device:TPU:8, one launch (start us, length us, event | category | flops | bytes accessed | tf_op | source)
XLA Modules:
  0.0 160.6 jit_solution(10946697809258414577)
XLA Ops:
  0.6 0.5 broadcast.3
  1.1 1.3 reduce.3
  2.5 0.1 reshape.14.owner
  2.6 0.0 copy-start
  2.6 1.8 %copy-done = f32[192,3840]{1,0:T(8,128)S(1)} copy-done((f32[192,3840]{1,0:T(8,128)S(1)}, f32[192,3840]{1,0:T(8,128)}, u32[]{:S(2)}) %copy-start) | copy-done | bytes 2949144
  4.4 0.0 copy-start.2
  4.4 0.9 copy-done.2
  5.3 13.0 %shard_map.77 = f32[32,192,128]{2,1,0:T(8,128)} custom-call(s32[16,16]{1,0:T(8,128)S(1)} %reshape.14.owner, s32[1]{0:T(128)} %bitcast.me, s32[256,128]{1,0:T(8,128)S(1)} %bitcast.9, f32[192,3840]{1,0:T(8,128)S(1)} %copy-done), custom_call_target="tpu_custom_call" | custom-call | tf_op jit(solution)/shard_map/pallas_call | solution.py:72
  18.3 87.7 %all_to_all.15.arrived = f32[32,192,128]{2,1,0:T(8,128)S(1)} all-to-all(f32[32,192,128]{2,1,0:T(8,128)} %shard_map.77), channel_id=1, replica_groups=mesh['child'=2,'row'=8,'col'=16] {'child','row'}, dimensions={0} | all-to-all | bytes 6291456 | tf_op jit(solution)/shard_map/all_to_all | solution.py:173
  106.0 0.0 copy-start.1
  106.0 9.8 %shard_map.78 = f32[8,192,128]{2,1,0:T(8,128)S(1)} custom-call(s32[16,16]{1,0:T(8,128)S(1)} %reshape.14.owner, s32[1]{0:T(128)} %bitcast.me, f32[32,192,128]{2,1,0:T(8,128)S(1)} %all_to_all.15.arrived, f32[2048,1024]{1,0:T(8,128)} %bitcast.10), custom_call_target="tpu_custom_call" | custom-call | tf_op jit(solution)/shard_map/pallas_call | solution.py:124
  115.8 0.0 copy-start.3
  115.8 27.5 %all_to_all.16.terms = f32[8,192,128]{2,1,0:T(8,128)S(1)} all-to-all(f32[8,192,128]{2,1,0:T(8,128)S(1)} %shard_map.78), channel_id=1, replica_groups=mesh['child'=2,'row'=8,'col'=16] {'row'}, dimensions={0} | all-to-all | bytes 1572864 | tf_op jit(solution)/shard_map/all_to_all | solution.py:175
  143.3 0.0 copy-done.1
  143.3 0.7 shard_map.79
  144.0 16.0 %all_to_all.17 = f32[16,64,128]{2,1,0:T(8,128)S(1)} all-to-all(f32[16,64,128]{2,1,0:T(8,128)S(1)} %get-tuple-element.5), channel_id=1, replica_groups=mesh['child'=2,'row'=8,'col'=16] {'col'}, dimensions={0} | all-to-all | bytes 1048576 | tf_op jit(solution)/shard_map/all_to_all | solution.py:177
  160.0 0.0 copy-done.3
  160.0 0.6 bitcast_subtract_fusion
  (1 shorter events, 0.0 us)
Async XLA Ops:
  2.6 1.8 %copy-start = (f32[192,3840]{1,0:T(8,128)S(1)}, f32[192,3840]{1,0:T(8,128)}, u32[]{:S(2)}) copy-start(f32[192,3840]{1,0:T(8,128)} %slab.1) | copy-start | bytes 8847364
  4.4 0.9 copy-start.2
  106.0 37.3 %copy-start.1 = (f32[1,192,1024]{2,1,0:T(8,128)S(1)}, f32[1,192,1024]{2,1,0:T(8,128)}, u32[]{:S(2)}) copy-start(f32[1,192,1024]{2,1,0:T(8,128)} %param.8) | copy-start | bytes 2359300
  115.8 44.2 %copy-start.3 = (f32[1,64,128]{2,1,0:T(8,128)S(1)}, f32[1,64,128]{2,1,0:T(8,128)}, u32[]{:S(2)}) copy-start(f32[1,64,128]{2,1,0:T(8,128)} %param.9) | copy-start | bytes 98308

commit v2 on v1

--- a/solution.py
+++ b/solution.py
@@ -1,3 +1,5 @@
+import functools
+
 import jax
 import jax.numpy as jnp
 from jax import lax
@@ -19,7 +21,16 @@
     return lax.dot_general(left, right, (contract, ((), ())), preferred_element_type=jnp.float32)
 
 
-def gather_kernel(owner, me, rows, slab, out, parts, tiles, slots):
+def rank_of(owner, block, tile, count):
+    own = owner[block, tile]
+
+    def earlier(other, rank):
+        return rank + jnp.where(owner[block, other] == own, 1, 0)
+
+    return lax.fori_loop(0, tile, earlier, 0)
+
+
+def gather_kernel(wanted, owner, me, rows, slab, out, parts, tiles, slots):
     slab_rows, width = slab.shape
     blocks, count = owner.shape
     high, low = split(slab[...])
@@ -30,10 +41,10 @@
     def block_scan(block, found):
         def tile_scan(tile, carry):
             found, rank = carry
-            hit = (owner[block, tile] == mine).astype(jnp.int32)
+            hit = owner[block, tile] == mine
             tiles[found] = block * count + tile
-            slots[found] = block * CAP + rank
-            return found + hit, rank + hit
+            slots[found] = block
+            return found + (hit & (rank == wanted)).astype(jnp.int32), rank + hit.astype(jnp.int32)
 
         return lax.fori_loop(0, count, tile_scan, (found, 0))[0]
 
@@ -63,43 +74,46 @@
     lax.fori_loop(0, (found + 1) // 2, pair, 0)
 
 
-def gather(parent_slab, rows, owner, me):
+def gather(wanted, parent_slab, rows, owner, me):
     slab_rows, width = parent_slab.shape
-    blocks, count = owner.shape
+    blocks = owner.shape[0]
     tile_len = rows.shape[1]
     smem = pl.BlockSpec(memory_space=pltpu.SMEM)
     vmem = pl.BlockSpec(memory_space=pltpu.VMEM)
     return pl.pallas_call(
-        gather_kernel,
-        out_shape=jax.ShapeDtypeStruct((blocks * CAP, slab_rows, tile_len), jnp.float32),
+        functools.partial(gather_kernel, wanted),
+        out_shape=jax.ShapeDtypeStruct((blocks, slab_rows, tile_len), jnp.float32),
         in_specs=[smem, smem, vmem, vmem],
         out_specs=vmem,
         scratch_shapes=[
             pltpu.VMEM((2 * slab_rows, width), jnp.bfloat16),
-            pltpu.SMEM((blocks * CAP + 8,), jnp.int32),
-            pltpu.SMEM((blocks * CAP + 8,), jnp.int32),
+            pltpu.SMEM((blocks + 8,), jnp.int32),
+            pltpu.SMEM((blocks + 8,), jnp.int32),
         ],
         compiler_params=pltpu.CompilerParams(vmem_limit_bytes=VMEM_LIMIT),
+        cost_estimate=pl.CostEstimate(flops=blocks * 4 * slab_rows * width * tile_len, bytes_accessed=8 << 20, transcendentals=0),
     )(owner, me, rows, parent_slab)
 
 
-def product_kernel(owner, me, arrived, panel, out, total):
+def triple(left, right):
+    left_high, left_low = split(left)
+    right_high, right_low = split(right)
+    return dot(
+        jnp.concatenate([left_high, left_high, left_low], axis=1),
+        jnp.concatenate([right_high, right_low, right_high], axis=0),
+    )
+
+
+def first_kernel(owner, me, arrived, panel, total):
     step = pl.program_id(0)
     count = owner.shape[1]
     mine = me[0]
 
-    def slot_of(tile):
-        own = owner[mine, tile]
-
-        def earlier(other, rank):
-            return rank + jnp.where((owner[mine, other] == own) & (other < tile), 1, 0)
-
-        return own * CAP + lax.fori_loop(0, count, earlier, 0)
-
-    left = jnp.concatenate([arrived[slot_of(2 * step)], arrived[slot_of(2 * step + 1)]], axis=1)
-    left_high, left_low = split(left)
-    right_high, right_low = split(panel[...])
-    term = dot(left_high, right_high) + dot(left_high, right_low) + dot(left_low, right_high)
+    def part(tile):
+        return jnp.where(rank_of(owner, mine, tile, count) == 0, arrived[owner[mine, tile]], 0.0)
+
+    left = jnp.concatenate([part(2 * step), part(2 * step + 1)], axis=1)
+    term = triple(left, panel[...])
 
     @pl.when(step == 0)
     def _():
@@ -109,32 +123,80 @@
     def _():
         total[...] -= term
 
-    @pl.when(step == pl.num_programs(0) - 1)
-    def _():
-        width = out.shape[2]
-        for block in range(out.shape[0]):
-            out[block] = total[:, block * width : (block + 1) * width]
-
-
-def product(arrived, panel, owner, me, blocks):
-    slots, slab_rows, tile_len = arrived.shape
+
+def first_product(arrived, panel, owner, me):
+    _, slab_rows, tile_len = arrived.shape
     panel_rows, width = panel.shape
     smem = pl.BlockSpec(memory_space=pltpu.SMEM)
-    out_shape = (blocks, slab_rows, width // blocks)
-    return pl.pallas_call(
-        product_kernel,
+    return pl.pallas_call(
+        first_kernel,
         grid=(panel_rows // (2 * tile_len),),
-        out_shape=jax.ShapeDtypeStruct(out_shape, jnp.float32),
+        out_shape=jax.ShapeDtypeStruct((slab_rows, width), jnp.float32),
         in_specs=[
             smem,
             smem,
             pl.BlockSpec(arrived.shape, lambda i: (0, 0, 0)),
             pl.BlockSpec((2 * tile_len, width), lambda i: (i, 0)),
         ],
-        out_specs=pl.BlockSpec(out_shape, lambda i: (0, 0, 0)),
-        scratch_shapes=[pltpu.VMEM((slab_rows, width), jnp.float32)],
-        compiler_params=pltpu.CompilerParams(vmem_limit_bytes=VMEM_LIMIT),
+        out_specs=pl.BlockSpec((slab_rows, width), lambda i: (0, 0)),
+        compiler_params=pltpu.CompilerParams(vmem_limit_bytes=VMEM_LIMIT),
+        cost_estimate=pl.CostEstimate(flops=6 * slab_rows * width * panel_rows, bytes_accessed=16 << 20, transcendentals=0),
     )(owner, me, arrived, panel)
+
+
+def second_kernel(groups, owner, me, first, arrived, panel, out, total, held, tiles, sems):
+    count = owner.shape[1]
+    tile_len = held.shape[1]
+    mine = me[0]
+
+    def copy(tile, place):
+        source = panel.at[pl.ds(pl.multiple_of(tile * tile_len, tile_len), tile_len), :]
+        return pltpu.make_async_copy(source, held.at[place], sems.at[place])
+
+    def scan(tile, found):
+        hit = rank_of(owner, mine, tile, count) == 1
+
+        @pl.when(hit)
+        def _():
+            tiles[found] = tile
+            copy(tile, found).start()
+
+        return found + hit.astype(jnp.int32)
+
+    found = lax.fori_loop(0, count, scan, 0)
+    total[...] = first[...]
+
+    def step(place, carry):
+        tile = tiles[place]
+        copy(tile, place).wait()
+        total[...] -= triple(arrived[lax.rem(owner[mine, tile], groups)], held[place])
+        return carry
+
+    lax.fori_loop(0, found, step, 0)
+    width = out.shape[2]
+    for block in range(out.shape[0]):
+        out[block] = total[:, block * width : (block + 1) * width]
+
+
+def second_product(first, arrived, panel, owner, me, blocks):
+    groups, slab_rows, tile_len = arrived.shape
+    width = panel.shape[1]
+    most = owner.shape[1] // CAP
+    smem = pl.BlockSpec(memory_space=pltpu.SMEM)
+    vmem = pl.BlockSpec(memory_space=pltpu.VMEM)
+    return pl.pallas_call(
+        functools.partial(second_kernel, groups),
+        out_shape=jax.ShapeDtypeStruct((blocks, slab_rows, width // blocks), jnp.float32),
+        in_specs=[smem, smem, vmem, vmem, pl.BlockSpec(memory_space=pl.ANY)],
+        out_specs=vmem,
+        scratch_shapes=[
+            pltpu.VMEM((slab_rows, width), jnp.float32),
+            pltpu.VMEM((most, tile_len, width), jnp.float32),
+            pltpu.SMEM((most + 8,), jnp.int32),
+            pltpu.SemaphoreType.DMA((most,)),
+        ],
+        compiler_params=pltpu.CompilerParams(vmem_limit_bytes=VMEM_LIMIT),
+    )(owner, me, first, arrived, panel)
 
 
 def diag_kernel(terms, slab_panel, inverse, out):
@@ -166,12 +228,32 @@
 def local(parent_slab, panel, slab_panel, diag_inverse, tile_rows, tile_owner):
     row_count, col_count = lax.axis_size("row"), lax.axis_size("col")
     group_size = lax.axis_size("child") * row_count
-    me = (lax.axis_index("child") * row_count + lax.axis_index("row")).astype(jnp.int32).reshape(1)
+    child = lax.axis_index("child")
+    me = (child * row_count + lax.axis_index("row")).astype(jnp.int32).reshape(1)
     owner = tile_owner.reshape(group_size, -1)
     rows = tile_rows.reshape(-1, tile_rows.shape[2])
-    columns = gather(parent_slab, rows, owner, me)
-    arrived = lax.all_to_all(columns, ("child", "row"), split_axis=0, concat_axis=0, tiled=True)
-    partial = product(arrived, panel[0], owner, me, row_count)
+    first_columns = gather(0, parent_slab, rows, owner, me)
+    first_arrived = lax.all_to_all(first_columns, ("child", "row"), split_axis=0, concat_axis=0, tiled=True)
+    second_columns = gather(1, parent_slab, rows, owner, me)
+    own = lax.dynamic_slice_in_dim(second_columns, child * row_count, row_count, 0)
+    other = lax.dynamic_slice_in_dim(second_columns, (1 - child) * row_count, row_count, 0)
+    passed = lax.ppermute(other, "child", [(0, 1), (1, 0)])
+    twice = jnp.sum((owner[:, :, None] == jnp.arange(group_size)).astype(jnp.int32), axis=1) > 1
+    mine = lax.dynamic_slice(twice, (child * row_count, me[0]), (row_count, 1))
+    merged = jnp.where(mine[:, :, None], own, passed)
+    single = ~jnp.any(twice[:, :row_count] & twice[:, row_count:])
+
+    def merged_sends(first_arrived, second_columns, merged):
+        arrived = lax.all_to_all(merged, "row", split_axis=0, concat_axis=0, tiled=True)
+        first = first_product(first_arrived, panel[0], owner, me)
+        return second_product(first, arrived, panel[0], owner, me, row_count)
+
+    def all_sends(first_arrived, second_columns, merged):
+        arrived = lax.all_to_all(second_columns, ("child", "row"), split_axis=0, concat_axis=0, tiled=True)
+        first = first_product(first_arrived, panel[0], owner, me)
+        return second_product(first, arrived, panel[0], owner, me, row_count)
+
+    partial = lax.cond(single, merged_sends, all_sends, first_arrived, second_columns, merged)
     terms = lax.all_to_all(partial, "row", split_axis=0, concat_axis=0, tiled=True)
     slab_inverse, parts = diag_terms(terms, slab_panel[0], col_count)
     reduced = lax.all_to_all(parts, "col", split_axis=0, concat_axis=0, tiled=True)

time: 161 us -> 142 us (0.88)
  blocking collectives: 131 us -> 43.3 us
  waiting for transfers between devices: 0 us -> 44.3 us
  starting transfers between devices: 0 us -> 14.7 us
  Pallas kernels: 23.5 us -> 28.3 us
  other arithmetic: 2 us -> 4.98 us
    all_to_all x1 -> x0, blocking collectives: 87.7 us -> none  [local(): lax.all_to_all(columns, ('child', 'row'), split_axis=0, concat_axis=0, ti...]
    all_to_all x0 -> x2, waiting for transfers between devices: none -> 44.3 us  [the longest x1 30.4 us: local(): lax.all_to_all(first_columns, ('child', 'row'), split_axis=0, concat_axis...]
    all_to_all x0 -> x2, starting transfers between devices: none -> 14.3 us  [the longest x1 8.97 us: local(): lax.all_to_all(first_columns, ('child', 'row'), split_axis=0, concat_axis...]
    pallas_call x2 -> x4, Pallas kernels: 22.8 us -> 27.6 us  [the longest x2 15.4 us: gather(): pl.pallas_call(functools.partial(gather_kernel, wanted), out_shape=jax.Sh...]
    select_n x0 -> x1, other arithmetic: none -> 2.17 us  [local(): merged = jnp.where(mine[:, :, None], own, passed)]
    unnamed x9 -> x15, local copies, waits for them, and re-layouts: 3.26 us -> 4.43 us
  transfers between devices with their start and end apart: 0 -> 3, of which waited for: 0 -> 2; matrix products, arithmetic and copies ran while one was open for 0% -> 1% of each run, Pallas kernels for 0% -> 9%
where the time goes in v2:
time: 142 us
  waiting for transfers between devices  44.3 us (31%)
  blocking collectives  43.3 us (30%)
  Pallas kernels  28.3 us (20%)
  starting transfers between devices  14.7 us (10%)
  other arithmetic  4.98 us (4%)
  local copies, waits for them, and re-layouts  4.72 us (3%)
    all_to_all x1, waiting for transfers between devices, local(): lax.all_to_all(first_columns, ('child', 'row'), split_axis=0, concat_axis...  30.4 us
    all_to_all x1, blocking collectives, local(): lax.all_to_all(partial, 'row', split_axis=0, concat_axis=0, tiled=True)  26.1 us
    all_to_all x1, blocking collectives, local(): lax.all_to_all(parts, 'col', split_axis=0, concat_axis=0, tiled=True)  17.2 us
    pallas_call x2, Pallas kernels, gather(): pl.pallas_call(functools.partial(gather_kernel, wanted), out_shape=jax.Sh...  15.4 us
    all_to_all x1, waiting for transfers between devices, merged_sends(): lax.all_to_all(merged, 'row', split_axis=0, concat_axis=0, tiled=True)  13.9 us
    pallas_call x1, Pallas kernels, first_product(): pl.pallas_call(first_kernel, grid=(panel_rows // (2 * tile_len),), out_sh...  9.33 us
    all_to_all x1, starting transfers between devices, local(): lax.all_to_all(first_columns, ('child', 'row'), split_axis=0, concat_axis...  8.97 us
    all_to_all x1, starting transfers between devices, merged_sends(): lax.all_to_all(merged, 'row', split_axis=0, concat_axis=0, tiled=True)  5.33 us
  transfers between devices with their start and end apart: 3, of which 2 were waited for; matrix products, arithmetic and copies ran while one was open for 1% of the time, Pallas kernels for 9%

profile of v2, /device:TPU:8, one launch (start us, length us, event | category | flops | bytes accessed | tf_op | source)
XLA Modules:
  0.0 141.7 jit_solution(2579978824651922745)
XLA Ops:
  0.6 0.5 broadcast.3
  1.1 1.3 reduce.3
  2.5 0.1 eq.15.owner
  2.6 1.8 %copy-done.1 = f32[192,3840]{1,0:T(8,128)S(1)} copy-done((f32[192,3840]{1,0:T(8,128)S(1)}, f32[192,3840]{1,0:T(8,128)}, u32[]{:S(2)}) %copy-start.1) | copy-done | bytes 2949144
  4.4 0.9 copy-done.3
  5.3 11.6 %shard_map.77 = f32[16,192,128]{2,1,0:T(8,128)} custom-call(s32[16,16]{1,0:T(8,128)S(1)} %eq.15.owner, s32[1]{0:T(128)} %bitcast.3.me, s32[256,128]{1,0:T(8,128)S(1)} %bitcast.12, f32[192,3840]{1,0:T(8,128)S(1)} %copy-done.1), custom_call_target="tpu_custom_call" | custom-call | flops 6039797760 | bytes 8388608 | tf_op jit(solution)/shard_map/pallas_call | solution.py:83
  17.0 9.0 %all-to-all-start.2 = ((f32[16,192,128]{2,1,0:T(8,128)}), f32[16,192,128]{2,1,0:T(8,128)}, u32[]{:S(2)}, u32[]{:S(2)}) async-start(f32[16,192,128]{2,1,0:T(8,128)} %shard_map.77), calls=%async_computation.2 | async-start | bytes 3145728 | tf_op jit(solution)/shard_map/all_to_all | solution.py:236
  26.0 3.8 %shard_map.78 = f32[16,192,128]{2,1,0:T(8,128)S(1)} custom-call(s32[16,16]{1,0:T(8,128)S(1)} %eq.15.owner, s32[1]{0:T(128)} %bitcast.3.me, s32[256,128]{1,0:T(8,128)S(1)} %bitcast.13, f32[192,3840]{1,0:T(8,128)S(1)} %copy-done.2), custom_call_target="tpu_custom_call" | custom-call | flops 6039797760 | bytes 8388608 | tf_op jit(solution)/shard_map/pallas_call | solution.py:83
  29.8 1.2 copy-done.5
  31.0 0.4 collective-permute-start
  31.4 0.1 convert_reduce_fusion
  31.5 0.7 fusion
  32.9 30.4 %all-to-all-done.2 = f32[16,192,128]{2,1,0:T(8,128)} async-done(((f32[16,192,128]{2,1,0:T(8,128)}), f32[16,192,128]{2,1,0:T(8,128)}, u32[]{:S(2)}, u32[]{:S(2)}) %all-to-all-start.2) | async-done | bytes 1572896 | tf_op jit(solution)/shard_map/all_to_all | solution.py:236
  63.3 33.7 %conditional.1 = (f32[8,192,128]{2,1,0:T(8,128)S(1)}) conditional(s32[]{:T(128)} %convert_element_type.7, (f32[1,2048,1024]{2,1,0:T(8,128)}, s32[16,16]{1,0:T(8,128)S(1)}, s32[1]{0:T(128)}, f32[16,192,128]{2,1,0:T(8,128)}, f32[16,192,128]{2,1,0:T(8,128)}) %tuple.20, (f32[1,2048,1024]{2,1,0:T(8,128)}, s32[16,16]{1,0:T(8,128)S(1)}, s32[1]{0:T(128)}, ...), branch_computations={%region_2.3_spmd, %region_3.4_spmd} | conditional | flops 2416115712 | bytes 21496460 | solution.py:256
  63.3 0.1 copy.8
  63.5 2.2 %dynamic-slice_select_fusion = f32[8,192,128]{2,1,0:T(8,128)} fusion(f32[8,192,128]{2,1,0:T(8,128)S(1)} %get-tuple-element.65, f32[16,192,128]{2,1,0:T(8,128)} %get-tuple-element.64, s32[]{:T(128)S(6)} %select_n.13, pred[8]{0:T(512)(128)(4,1)S(1)} %dynamic-slice_bitcast_fusion), kind=kLoop, calls=%fused_computation | loop fusion | flops 196608 | bytes 2359308 | tf_op jit(solution)/shard_map/jit(_where)/select_n | solution.py:243
  65.6 5.3 %all-to-all-start.1 = ((f32[8,192,128]{2,1,0:T(8,128)}), f32[8,192,128]{2,1,0:T(8,128)S(1)}, u32[]{:S(2)}, u32[]{:S(2)}) async-start(f32[8,192,128]{2,1,0:T(8,128)} %dynamic-slice_select_fusion), calls=%async_computation.1 | async-start | bytes 1572864 | tf_op jit(solution)/shard_map/cond/branch_1_fun/all_to_all | solution.py:247
  71.0 9.3 %branch_1_fun.2.first = f32[192,1024]{1,0:T(8,128)S(1)} custom-call(s32[16,16]{1,0:T(8,128)S(1)} %get-tuple-element.57.owner, s32[1]{0:T(128)} %get-tuple-element.58.me, f32[16,192,128]{2,1,0:T(8,128)} %get-tuple-element.59.arrived, f32[2048,1024]{1,0:T(8,128)} %bitcast.16), custom_call_target="tpu_custom_call" | custom-call | flops 2415919104 | bytes 16777216 | tf_op jit(solution)/shard_map/cond/branch_1_fun/pallas_call | solution.py:131
  80.3 13.9 %all-to-all-done.1.arrived = f32[8,192,128]{2,1,0:T(8,128)S(1)} async-done(((f32[8,192,128]{2,1,0:T(8,128)}), f32[8,192,128]{2,1,0:T(8,128)S(1)}, u32[]{:S(2)}, u32[]{:S(2)}) %all-to-all-start.1) | async-done | bytes 786464 | tf_op jit(solution)/shard_map/cond/branch_1_fun/all_to_all | solution.py:247
  94.2 2.8 %branch_1_fun.3 = f32[8,192,128]{2,1,0:T(8,128)S(1)} custom-call(s32[16,16]{1,0:T(8,128)S(1)} %get-tuple-element.57.owner, s32[1]{0:T(128)} %get-tuple-element.58.me, f32[192,1024]{1,0:T(8,128)S(1)} %branch_1_fun.2.first, f32[8,192,128]{2,1,0:T(8,128)S(1)} %all-to-all-done.1.arrived, f32[2048,1024]{1,0:T(8,128)} %bitcast.17), custom_call_target="tpu_custom_call" | custom-call | tf_op jit(solution)/shard_map/cond/branch_1_fun/pallas_call | solution.py:187
  97.0 26.1 %all_to_all.23.terms = f32[8,192,128]{2,1,0:T(8,128)S(1)} all-to-all(f32[8,192,128]{2,1,0:T(8,128)S(1)} %get-tuple-element.81), channel_id=1, replica_groups=mesh['child'=2,'row'=8,'col'=16] {'row'}, dimensions={0} | all-to-all | bytes 1572864 | tf_op jit(solution)/shard_map/all_to_all | solution.py:257
  123.1 0.7 shard_map.79
  123.8 17.2 %all_to_all.24 = f32[16,64,128]{2,1,0:T(8,128)S(1)} all-to-all(f32[16,64,128]{2,1,0:T(8,128)S(1)} %get-tuple-element.71), channel_id=1, replica_groups=mesh['child'=2,'row'=8,'col'=16] {'col'}, dimensions={0} | all-to-all | bytes 1048576 | tf_op jit(solution)/shard_map/all_to_all | solution.py:259
  141.1 0.6 bitcast_subtract_fusion
  (16 shorter events, 0.2 us)
Async XLA Ops:
  2.6 1.8 %copy-start.1 = (f32[192,3840]{1,0:T(8,128)S(1)}, f32[192,3840]{1,0:T(8,128)}, u32[]{:S(2)}) copy-start(f32[192,3840]{1,0:T(8,128)} %slab.3) | copy-start | bytes 8847364
  4.4 0.9 copy-start.3
  17.0 9.0 %copy-start.2 = (f32[192,3840]{1,0:T(8,128)S(1)}, f32[192,3840]{1,0:T(8,128)}, u32[]{:S(2)}) copy-start(f32[192,3840]{1,0:T(8,128)} %slab.3) | copy-start | bytes 8847364
  17.0 9.0 %copy-start.4 = (s32[2,128,128]{2,1,0:T(8,128)S(1)}, s32[2,128,128]{2,1,0:T(8,128)}, u32[]{:S(2)}) copy-start(s32[2,128,128]{2,1,0:T(8,128)} %param.12) | copy-start | bytes 393220
  17.0 46.3 %all-to-all-start.2 = ((f32[16,192,128]{2,1,0:T(8,128)}), f32[16,192,128]{2,1,0:T(8,128)}, u32[]{:S(2)}, u32[]{:S(2)}) async-start(f32[16,192,128]{2,1,0:T(8,128)} %shard_map.77), calls=%async_computation.2 | async-start | bytes 3145728 | tf_op jit(solution)/shard_map/all_to_all | solution.py:236
  29.7 1.2 copy-start.5
  31.0 32.3 %collective-permute-start = (f32[8,192,128]{2,1,0:T(8,128)S(1)}, f32[8,192,128]{2,1,0:T(8,128)S(1)}, u32[]{:S(2)}, u32[]{:S(2)}) collective-permute-start(f32[8,192,128]{2,1,0:T(8,128)S(1)} %constant_dynamic-slice_fusion), channel_id=1, source_target_pairs={{0,128},{128,0},{1,129},{129,1},{2,130},{130,2},{3,131},{131,3},{4... | collective-permute-start | bytes 2359304 | tf_op jit(solution)/shard_map/ppermute | solution.py:240
  65.6 28.6 %all-to-all-start.1 = ((f32[8,192,128]{2,1,0:T(8,128)}), f32[8,192,128]{2,1,0:T(8,128)S(1)}, u32[]{:S(2)}, u32[]{:S(2)}) async-start(f32[8,192,128]{2,1,0:T(8,128)} %dynamic-slice_select_fusion), calls=%async_computation.1 | async-start | bytes 1572864 | tf_op jit(solution)/shard_map/cond/branch_1_fun/all_to_all | solution.py:247
  97.0 26.1 %copy-start = (f32[1,192,1024]{2,1,0:T(8,128)S(1)}, f32[1,192,1024]{2,1,0:T(8,128)}, u32[]{:S(2)}) copy-start(f32[1,192,1024]{2,1,0:T(8,128)} %param.10) | copy-start | bytes 2359300
  123.1 18.0 %copy-start.6 = (f32[1,64,128]{2,1,0:T(8,128)S(1)}, f32[1,64,128]{2,1,0:T(8,128)}, u32[]{:S(2)}) copy-start(f32[1,64,128]{2,1,0:T(8,128)} %param.11) | copy-start | bytes 98308
